TPU v7x, 256 devices: a whole 4x4x8 slice. The times are simulated.
256 devices in a mesh: dp: 8 (over x, z_lo), ctx: 32 (over y, z_hi, core).
Axes of the slice: x: 4, y: 4, z: 8 (z_hi: 4, z_lo: 2; z = z_hi * 2 + z_lo), core: 2. Of those that a mesh axis runs over, the one named last changes fastest.
Arguments:
- queries: bfloat16 [32768, 8192], P(('dp', 'ctx')), may hold values from -16 to 16
- out_grad: bfloat16 [32768, 8192], P(('dp', 'ctx')), may hold values from -6 to 6
- enc_states: bfloat16 [3072, 1024], P(('dp', 'ctx')), may hold values from -8 to 8
- w_key: bfloat16 [1024, 8192], P('dp', 'ctx'), may hold values from -1 to 1
- w_value: bfloat16 [1024, 8192], P('dp', 'ctx'), may hold values from -0.1875 to 0.1875
- dec_segments: int32 [32768], P(('dp', 'ctx')), may hold values from 0 to 3, as said below
- enc_segments: int32 [3072], P(('dp', 'ctx')), may hold values from 0 to 3, as said below
Outputs:
- query_grad: bfloat16 [32768, 8192], P(('dp', 'ctx'))
- enc_grad: bfloat16 [3072, 1024], P(('dp', 'ctx'))
- w_key_grad: float32 [1024, 8192], P('dp', 'ctx')
- w_value_grad: float32 [1024, 8192], P('dp', 'ctx')
Inputs may be any that keep to these rules, and one draw needn't show every extreme that they name: `dec_segments`: within each pack the ids never fall along the tokens, and each of the 4 ids has one or more decoder tokens in the pack. `enc_segments`: within each pack the ids never fall along the tokens, and each of the 4 ids has two or more encoder tokens in the pack.
All inputs are finite; a program needn't handle non-finite values.
Results may differ from a plain program's by a relative error of at most 0.019.
Values may be sent and summed in bfloat16 or wider, within the bound.
No kernel may reach another device: no remote copies, remote signals or barrier semaphores. Data moves between devices by JAX's collectives and lax.ppermute only.
A program may use at most 64 MiB of HBM per device.

v0:
```python
import math
import jax
import jax.numpy as jnp
from jax import lax
from jax.sharding import PartitionSpec as P

HEAD_DIM = 128


def side_by_side(arrays, axis, dim, along):
    ends, at = ([], 0)
    for a in arrays[:-1]:
        at += a.shape[along]
        ends.append(at)
    both = jnp.concatenate(arrays, axis=along)
    return tuple(jnp.split(lax.all_gather(both, axis, axis=dim, tiled=True), ends, axis=along))


def sent_to_all(value, axis):
    size = lax.axis_size(axis)
    return lax.all_to_all(
        jnp.broadcast_to(value[None], (size, *value.shape)), axis, 0, 0, tiled=True
    )


def joined_along(pieces, dim):
    pieces = jnp.moveaxis(pieces, 0, dim)
    lengths = pieces.shape
    return pieces.reshape(*lengths[:dim], lengths[dim] * lengths[dim + 1], *lengths[dim + 2 :])


def gathered_copies(value, axis, dim):
    pieces = sent_to_all(value, axis)
    return joined_along(pieces, dim)


def split_up(value, dim, size):
    lengths = value.shape
    pieces = value.reshape(*lengths[:dim], size, lengths[dim] // size, *lengths[dim + 1 :])
    return jnp.moveaxis(pieces, dim, 0)


def sum_at_owner(value, axis, dim):
    pieces = split_up(value, dim, lax.axis_size(axis))
    arrived = lax.all_to_all(pieces, axis, split_axis=0, concat_axis=0, tiled=True)
    return arrived.astype(jnp.float32).sum(axis=0)


def in_one_piece(arrays, axis, dim, along):
    ends, at = ([], 0)
    for a in arrays[:-1]:
        at += a.shape[along]
        ends.append(at)
    both = jnp.concatenate(arrays, axis=along)
    return tuple(
        jnp.split(lax.psum_scatter(both, axis, scatter_dimension=dim, tiled=True), ends, axis=along)
    )


def attend(queries, out_grads, key_rows, value_rows, query_ids, key_ids):
    length, full_width = queries.shape
    key_count = key_rows.shape[0]
    head_count = full_width // HEAD_DIM
    group_size = min(head_count, 16)
    column_count = group_size * HEAD_DIM
    row_count = math.gcd(length, 1024)

    def head_group(number):
        column_start = number * column_count
        key_block = key_rows.reshape(key_count, group_size, HEAD_DIM)
        value_block = value_rows.reshape(key_count, group_size, HEAD_DIM)

        def query_block(totals, block_number):
            first_row = block_number * row_count
            query_part = lax.dynamic_slice(
                queries, (first_row, column_start), (row_count, column_count)
            ).reshape(row_count, group_size, HEAD_DIM)
            grad_part = lax.dynamic_slice(
                out_grads, (first_row, column_start), (row_count, column_count)
            ).reshape(row_count, group_size, HEAD_DIM)
            block_ids = lax.dynamic_slice_in_dim(query_ids, first_row, row_count, 0)
            allowed = block_ids[:, None] == key_ids[None, :]
            scores = jnp.einsum(
                "qhd,khd->hqk", query_part, key_block, preferred_element_type=jnp.float32
            )
            scores = jnp.where(allowed[None], scores, -jnp.inf)
            highest = jnp.max(scores, axis=2, keepdims=True)
            weights = jnp.exp(scores - highest)
            probability = weights / jnp.sum(weights, axis=2, keepdims=True)
            upstream = jnp.einsum(
                "qhd,khd->hqk", grad_part, value_block, preferred_element_type=jnp.float32
            )
            row_dot = jnp.sum(probability * upstream, axis=2, keepdims=True)
            score_grad = (probability * (upstream - row_dot)).astype(jnp.bfloat16)
            rounded = probability.astype(jnp.bfloat16)
            key_total = totals[0] + jnp.einsum(
                "hqk,qhd->khd", score_grad, query_part, preferred_element_type=jnp.float32
            )
            value_total = totals[1] + jnp.einsum(
                "hqk,qhd->khd", rounded, grad_part, preferred_element_type=jnp.float32
            )
            totals = (key_total, value_total)
            query_grad = jnp.einsum(
                "hqk,khd->qhd", score_grad, key_block, preferred_element_type=jnp.float32
            ).astype(jnp.bfloat16)
            return (totals, query_grad.reshape(row_count, column_count))

        zeros = jnp.zeros((key_count, group_size, HEAD_DIM), jnp.float32)
        totals, query_grads = lax.scan(
            query_block, (zeros, zeros), jnp.arange(length // row_count, dtype=jnp.int32)
        )
        results = ()
        results = results + (query_grads.reshape(length, column_count),)
        results = results + (
            totals[0].reshape(key_count, column_count),
            totals[1].reshape(key_count, column_count),
        )
        return results

    pieces = lax.map(head_group, jnp.arange(head_count // group_size, dtype=jnp.int32))
    return tuple(
        (jnp.moveaxis(piece, 0, 1).reshape(piece.shape[1], full_width) for piece in pieces)
    )


def body(queries, out_grad, enc_states, w_key, w_value, dec_segments, enc_segments):
    encoder, key_ids = (
        lax.all_gather(enc_states, "ctx", axis=0, tiled=True),
        lax.all_gather(enc_segments, "ctx", axis=0, tiled=True),
    )
    key_weight, value_weight = side_by_side((w_key, w_value), "dp", 0, 1)
    key_part = jnp.dot(encoder, key_weight, preferred_element_type=jnp.float32).astype(jnp.bfloat16)
    value_part = jnp.dot(encoder, value_weight, preferred_element_type=jnp.float32).astype(
        jnp.bfloat16
    )
    local_queries, local_grads = (
        lax.all_to_all(queries, "ctx", split_axis=1, concat_axis=0, tiled=True),
        lax.all_to_all(out_grad, "ctx", split_axis=1, concat_axis=0, tiled=True),
    )
    query_ids = gathered_copies(dec_segments, "ctx", 0)
    head_grad, key_grad, value_grad = attend(
        local_queries, local_grads, key_part, value_part, query_ids, key_ids
    )
    query_grad = lax.all_to_all(head_grad, "ctx", split_axis=0, concat_axis=1, tiled=True)
    key_round = key_grad.astype(jnp.bfloat16)
    value_round = value_grad.astype(jnp.bfloat16)
    across = (((1,), (1,)), ((), ()))
    partial_value = lax.dot_general(
        key_round, key_weight, across, preferred_element_type=jnp.float32
    )
    partial_value = partial_value + lax.dot_general(
        value_round, value_weight, across, preferred_element_type=jnp.float32
    )
    enc_grad = sum_at_owner(partial_value.astype(jnp.bfloat16), "ctx", 0).astype(jnp.bfloat16)
    down = (((0,), (0,)), ((), ()))
    key_term = lax.dot_general(encoder, key_round, down, preferred_element_type=jnp.float32)
    value_term = lax.dot_general(encoder, value_round, down, preferred_element_type=jnp.float32)
    w_key_grad, w_value_grad = tuple(
        (
            part.astype(jnp.float32)
            for part in in_one_piece(
                (key_term.astype(jnp.bfloat16), value_term.astype(jnp.bfloat16)), "dp", 0, 1
            )
        )
    )
    return (query_grad, enc_grad, w_key_grad, w_value_grad)


def solution(mesh):
    in_specs = (
        P(("dp", "ctx"), None),
        P(("dp", "ctx"), None),
        P(("dp", "ctx"), None),
        P("dp", "ctx"),
        P("dp", "ctx"),
        P(("dp", "ctx")),
        P(("dp", "ctx")),
    )
    out_specs = (P(("dp", "ctx"), None), P(("dp", "ctx"), None), P("dp", "ctx"), P("dp", "ctx"))
    return jax.shard_map(body, mesh=mesh, in_specs=in_specs, out_specs=out_specs, check_vma=False)
```

profile of v0, /device:TPU:8, one launch (start us, length us, event | category | flops | bytes accessed | tf_op | source)
XLA Modules:
  0.0 417.5 jit_solution(9430888007886917703)
XLA Ops:
  7.2 4.1 copy.68
  11.2 11.7 %all-to-all-start = ((bf16[128,32,256]{0,2,1:T(8,128)(2,1)}), bf16[128,32,256]{0,2,1:T(8,128)(2,1)S(1)}, u32[]{:S(2)}, u32[]{:S(2)}) async-start(bf16[128,32,256]{0,2,1:T(8,128)(2,1)} %bitcast.99), calls=%async_computation | async-start | bytes 4194304 | tf_op jit(solution)/shard_map/all_to_all | solution.py:137
  22.9 4.1 copy.70
  27.1 44.4 %all-to-all-done = bf16[128,32,256]{0,2,1:T(8,128)(2,1)S(1)} async-done(((bf16[128,32,256]{0,2,1:T(8,128)(2,1)}), bf16[128,32,256]{0,2,1:T(8,128)(2,1)S(1)}, u32[]{:S(2)}, u32[]{:S(2)}) %all-to-all-start) | async-done | bytes 2097184 | tf_op jit(solution)/shard_map/all_to_all | solution.py:137
  71.4 1.3 copy-done.4
  72.8 7.6 %all-to-all-start.2 = ((bf16[128,32,256]{0,2,1:T(8,128)(2,1)}), bf16[128,32,256]{0,2,1:T(8,128)(2,1)}, u32[]{:S(2)}, u32[]{:S(2)}) async-start(bf16[128,32,256]{0,2,1:T(8,128)(2,1)} %bitcast.97), calls=%async_computation.2 | async-start | bytes 4194304 | tf_op jit(solution)/shard_map/all_to_all | solution.py:138
  81.2 96.0 %all-gather = bf16[32,12,1024]{2,1,0:T(8,128)(2,1)S(1)} all-gather(bf16[1,12,1024]{2,1,0:T(8,128)(2,1)S(1)} %bitcast.108), channel_id=1, replica_groups=mesh['dp'=8,'ctx'=32] {'ctx'}, dimensions={0}, use_global_device_ids=true | all-gather | bytes 811008 | tf_op jit(solution)/shard_map/all_gather | solution.py:128
  179.1 17.7 %all-reduce = s32[384]{0:T(512)S(1)} all-reduce(s32[384]{0:T(512)S(1)} %dynamic-update-slice), channel_id=1, replica_groups=mesh['dp'=8,'ctx'=32] {'ctx'}, use_global_device_ids=true, to_apply=%add | all-reduce | flops 384 | bytes 3072
  196.8 1.5 convolution_convert_fusion.3
  199.0 10.4 %all-to-all-start.1 = ((s32[32,1,128]{2,1,0:T(1,128)}), s32[32,1,128]{2,1,0:T(1,128)}, u32[]{:S(2)}, u32[]{:S(2)}) async-start(s32[32,1,128]{2,1,0:T(1,128)} %broadcast_in_dim.41), calls=%async_computation.1 | async-start | bytes 32768 | tf_op jit(solution)/shard_map/all_to_all | solution.py:21
  209.4 2.2 convolution_convert_fusion.4
  212.4 3.3 copy.69
  215.7 4.1 copy.71
  219.8 62.6 %while.27 = (s32[]{:T(128)}, f32[384,2,128]{0,2,1:T(8,128)S(1)}, f32[384,2,128]{0,2,1:T(8,128)}, bf16[4,1024,256]{2,1,0:T(8,128)(2,1)}, s32[4]{0:T(128)S(1)}, /*...) while((s32[]{:T(128)}, f32[384,2,128]{0,2,1:T(8,128)S(1)}, ...), condition=%wide.region_4.5_spmd.clone, body=%wide.region_0.4_spmd.clone.sunk | while | flops 1017117056 | bytes 58062732 | solution.py:109
  222.9 1.1 constant_dynamic-slice_fusion.3
  226.1 2.5 fusion.69
  228.7 2.6 fusion.71
  238.5 1.1 constant_dynamic-slice_fusion.3
  241.6 2.5 fusion.69
  244.2 2.7 fusion.71
  254.2 1.1 constant_dynamic-slice_fusion.3
  257.3 2.5 fusion.69
  259.9 2.7 fusion.71
  273.0 2.5 fusion.69
  275.6 2.7 fusion.71
  283.5 1.5 fusion.22
  285.6 36.9 %all_to_all.68 = bf16[32,12,1024]{2,1,0:T(8,128)(2,1)} all-to-all(bf16[32,12,1024]{2,1,0:T(8,128)(2,1)S(1)} %reshape.98), channel_id=1, replica_groups=mesh['dp'=8,'ctx'=32] {'ctx'}, dimensions={0} | all-to-all | bytes 1572864 | tf_op jit(solution)/shard_map/all_to_all | solution.py:45
  322.5 6.9 %all-to-all-start.3 = ((bf16[32,128,256]{2,1,0:T(8,128)(2,1)}), bf16[32,128,256]{2,1,0:T(8,128)(2,1)S(1)}, u32[]{:S(2)}, u32[]{:S(2)}) async-start(bf16[32,128,256]{2,1,0:T(8,128)(2,1)} %bitcast.102), calls=%async_computation.3 | async-start | bytes 4194304 | tf_op jit(solution)/shard_map/all_to_all | solution.py:144
  331.5 2.4 copy.86
  334.7 66.3 %reduce-scatter.4.cloned.1.call-done = bf16[128,512]{1,0:T(8,128)(2,1)} async-done(((bf16[1024,512]{1,0:T(8,128)(2,1)}), bf16[128,512]{1,0:T(8,128)(2,1)}) %reduce-scatter.4.cloned.1.call-update) | async-done | bytes 131088
  403.7 2.9 copy.76
  406.6 4.1 copy.77
  (146 shorter events, 46.0 us)
Async XLA Ops:
  11.2 60.2 %all-to-all-start = ((bf16[128,32,256]{0,2,1:T(8,128)(2,1)}), bf16[128,32,256]{0,2,1:T(8,128)(2,1)S(1)}, u32[]{:S(2)}, u32[]{:S(2)}) async-start(bf16[128,32,256]{0,2,1:T(8,128)(2,1)} %bitcast.99), calls=%async_computation | async-start | bytes 4194304 | tf_op jit(solution)/shard_map/all_to_all | solution.py:137
  71.4 9.0 %copy-start.11 = (bf16[128,256]{1,0:T(8,128)(2,1)S(1)}, bf16[128,256]{1,0:T(8,128)(2,1)}, u32[]{:S(2)}) copy-start(bf16[128,256]{1,0:T(8,128)(2,1)} %param.13) | copy-start | bytes 196612
  71.4 9.1 %copy-start.12 = (bf16[128,256]{1,0:T(8,128)(2,1)S(1)}, bf16[128,256]{1,0:T(8,128)(2,1)}, u32[]{:S(2)}) copy-start(bf16[128,256]{1,0:T(8,128)(2,1)} %param.12) | copy-start | bytes 196612
  71.4 9.8 %copy-start.13 = (bf16[12,1024]{1,0:T(8,128)(2,1)S(1)}, bf16[12,1024]{1,0:T(8,128)(2,1)}, u32[]{:S(2)}) copy-start(bf16[12,1024]{1,0:T(8,128)(2,1)} %param.11) | copy-start | bytes 73732
  72.8 125.6 %all-to-all-start.2 = ((bf16[128,32,256]{0,2,1:T(8,128)(2,1)}), bf16[128,32,256]{0,2,1:T(8,128)(2,1)}, u32[]{:S(2)}, u32[]{:S(2)}) async-start(bf16[128,32,256]{0,2,1:T(8,128)(2,1)} %bitcast.97), calls=%async_computation.2 | async-start | bytes 4194304 | tf_op jit(solution)/shard_map/all_to_all | solution.py:138
  80.4 97.1 %copy-start.16 = (u32[256]{0:T(256)S(1)}, u32[256]{0:T(256)}, u32[]{:S(2)}) copy-start(u32[256]{0:T(256)} %constant.64) | copy-start | bytes 3076
  80.4 98.4 %copy-start.15 = (s32[12]{0:T(128)S(1)}, s32[12]{0:T(128)}, u32[]{:S(2)}) copy-start(s32[12]{0:T(128)} %param.15) | copy-start | bytes 148
  80.4 116.4 %all-gather.3.cloned.1.call-start = ((), (), s32[]{:S(2)}) async-start(), calls=%async_computation.6 | async-start | bytes 1179648 | tf_op jit(solution)/shard_map/all_gather | solution.py:16
  81.2 117.1 %copy-start.14 = (s32[128]{0:T(128)S(1)}, s32[128]{0:T(128)}, u32[]{:S(2)}) copy-start(s32[128]{0:T(128)} %param.14) | copy-start | bytes 1540
  177.5 38.2 %copy-start.5 = (bf16[384,1024]{1,0:T(8,128)(2,1)}, bf16[384,1024]{1,0:T(8,128)(2,1)S(1)}, u32[]{:S(2)}) copy-start(bf16[384,1024]{1,0:T(8,128)(2,1)S(1)} %reshape.103) | copy-start | bytes 2359300
  199.0 20.8 %all-to-all-start.1 = ((s32[32,1,128]{2,1,0:T(1,128)}), s32[32,1,128]{2,1,0:T(1,128)}, u32[]{:S(2)}, u32[]{:S(2)}) async-start(s32[32,1,128]{2,1,0:T(1,128)} %broadcast_in_dim.41), calls=%async_computation.1 | async-start | bytes 32768 | tf_op jit(solution)/shard_map/all_to_all | solution.py:21
  219.8 6.3 %copy-start.2 = (bf16[4096,256]{1,0:T(8,128)(2,1)}, bf16[4096,256]{1,0:T(8,128)(2,1)S(1)}, u32[]{:S(2)}) copy-start(bf16[4096,256]{1,0:T(8,128)(2,1)S(1)} %get-tuple-element.377) | copy-start | bytes 6291460 | tf_op jit(solution)/shard_map/while/body/eval_jaxpr/while
  228.6 2.6 copy-start.1
  228.6 2.6 copy-start.10
  233.8 1.6 copy-start.3
  235.4 6.3 %copy-start.2 = (bf16[4096,256]{1,0:T(8,128)(2,1)}, bf16[4096,256]{1,0:T(8,128)(2,1)S(1)}, u32[]{:S(2)}) copy-start(bf16[4096,256]{1,0:T(8,128)(2,1)S(1)} %get-tuple-element.377) | copy-start | bytes 6291460 | tf_op jit(solution)/shard_map/while/body/eval_jaxpr/while
  244.2 2.7 copy-start.1
  244.2 2.7 copy-start.10
  249.4 1.6 copy-start.3
  251.0 6.3 %copy-start.2 = (bf16[4096,256]{1,0:T(8,128)(2,1)}, bf16[4096,256]{1,0:T(8,128)(2,1)S(1)}, u32[]{:S(2)}) copy-start(bf16[4096,256]{1,0:T(8,128)(2,1)S(1)} %get-tuple-element.377) | copy-start | bytes 6291460 | tf_op jit(solution)/shard_map/while/body/eval_jaxpr/while
  259.9 2.7 copy-start.1
  259.9 2.7 copy-start.10
  265.1 1.6 copy-start.3
  266.7 6.3 %copy-start.2 = (bf16[4096,256]{1,0:T(8,128)(2,1)}, bf16[4096,256]{1,0:T(8,128)(2,1)S(1)}, u32[]{:S(2)}) copy-start(bf16[4096,256]{1,0:T(8,128)(2,1)S(1)} %get-tuple-element.377) | copy-start | bytes 6291460 | tf_op jit(solution)/shard_map/while/body/eval_jaxpr/while
  275.5 2.7 copy-start.1
  275.6 2.7 copy-start.10
  280.8 1.6 copy-start.3
  282.4 2.6 copy-start.9
  322.5 7.0 %copy-start.6 = (bf16[384,1024]{1,0:T(8,128)(2,1)S(1)}, bf16[384,1024]{1,0:T(8,128)(2,1)}, u32[]{:S(2)}) copy-start(bf16[384,1024]{1,0:T(8,128)(2,1)} %copy-done.5) | copy-start | bytes 2359300
  322.5 81.2 %all-to-all-start.3 = ((bf16[32,128,256]{2,1,0:T(8,128)(2,1)}), bf16[32,128,256]{2,1,0:T(8,128)(2,1)S(1)}, u32[]{:S(2)}, u32[]{:S(2)}) async-start(bf16[32,128,256]{2,1,0:T(8,128)(2,1)} %bitcast.102), calls=%async_computation.3 | async-start | bytes 4194304 | tf_op jit(solution)/shard_map/all_to_all | solution.py:144
  329.5 71.6 %reduce-scatter.4.cloned.1.call-start = ((), (), s32[]{:S(2)}) async-start(), calls=%async_computation.7 | async-start | bytes 1179648
  331.5 2.4 copy-start.8
  (9 other events, 9.2 us)
Sparse Core Ops, SparseCore 0:
  83.6 70.4 all-gather.2
  334.0 66.9 reduce-scatter.3
where the time goes:
time: 419 us; the launch traced here: 417 us
  blocking collectives  151 us (36%)
  waiting for transfers between devices  111 us (26%)
  local copies, waits for them, and re-layouts  56.4 us (13%)
  starting transfers between devices  36.7 us (9%)
  matrix products  33.8 us (8%)
  between operations  15 us (4%)
  other arithmetic  11.1 us (3%)
    all_gather x1, blocking collectives, body(): lax.all_gather(enc_states, 'ctx', axis=0, tiled=True)  96 us
    unnamed x3, waiting for transfers between devices  66.4 us
    all_to_all x1, waiting for transfers between devices, body(): lax.all_to_all(queries, 'ctx', split_axis=1, concat_axis=0, tiled=True)  44.4 us
    all_to_all x1, blocking collectives, sum_at_owner(): lax.all_to_all(pieces, axis, split_axis=0, concat_axis=0, tiled=True)  36.9 us
    unnamed x35, local copies, waits for them, and re-layouts  19.7 us
    unnamed x1, blocking collectives  17.7 us
    all_to_all x1, starting transfers between devices, body(): lax.all_to_all(queries, 'ctx', split_axis=1, concat_axis=0, tiled=True)  11.7 us
    dot_general x4, matrix products, query_block(): jnp.einsum('hqk,qhd->khd', rounded, grad_part, preferred_element_type=jnp...  10.5 us
  transfers between devices with their start and end apart: 6, of which 2 were waited for; matrix products, arithmetic and copies ran while one was open for 6% of the time, Pallas kernels for 0%

commit v1 on v0

--- a/solution.py
+++ b/solution.py
@@ -3,6 +3,7 @@
 import jax.numpy as jnp
 from jax import lax
 from jax.sharding import PartitionSpec as P
+from jax.lax import all_to_all, axis_size
 
 HEAD_DIM = 128
 
@@ -124,8 +125,16 @@
 
 
 def body(queries, out_grad, enc_states, w_key, w_value, dec_segments, enc_segments):
+
+    def prepare_cards_here(m):
+        state_now = axis_size("ctx")
+        v_next = jnp.stack([m] * state_now, axis=0)
+        e_now = all_to_all(v_next, "ctx", 0, 0)
+        n_now = jnp.concatenate(e_now, axis=0)
+        return n_now
+
     encoder, key_ids = (
-        lax.all_gather(enc_states, "ctx", axis=0, tiled=True),
+        prepare_cards_here(enc_states),
         lax.all_gather(enc_segments, "ctx", axis=0, tiled=True),
     )
     key_weight, value_weight = side_by_side((w_key, w_value), "dp", 0, 1)

time: 419 us -> 406 us (0.969)
  blocking collectives: 151 us -> 106 us
  waiting for transfers between devices: 111 us -> 137 us
  starting transfers between devices: 36.7 us -> 41.1 us
    all_gather x1 -> x0, blocking collectives: 96 us -> none  [body(): lax.all_gather(enc_states, 'ctx', axis=0, tiled=True)]
    unnamed x1, blocking collectives: 17.7 us -> 69 us
    all_to_all x0 -> x1, waiting for transfers between devices: none -> 25.2 us  [prepare_cards_here(): e_now = all_to_all(v_next, 'ctx', 0, 0)]
    all_to_all x0 -> x1, starting transfers between devices: none -> 11.7 us  [prepare_cards_here(): e_now = all_to_all(v_next, 'ctx', 0, 0)]
    all_to_all x1, starting transfers between devices: 11.7 us -> 6.65 us  [body(): lax.all_to_all(queries, 'ctx', split_axis=1, concat_axis=0, tiled=True)]
    unnamed x35 -> x34, local copies, waits for them, and re-layouts: 19.7 us -> 17.8 us
  transfers between devices with their start and end apart: 6 -> 7, of which waited for: 2 -> 3; matrix products, arithmetic and copies ran while one was open for 6% -> 7% of each run, Pallas kernels for 0% -> 0%
where the time goes in v1:
time: 406 us; the launch traced here: 404 us
  waiting for transfers between devices  137 us (34%)
  blocking collectives  106 us (26%)
  local copies, waits for them, and re-layouts  56.5 us (14%)
  starting transfers between devices  41.1 us (10%)
  matrix products  34.1 us (8%)
  between operations  15 us (4%)
  other arithmetic  11 us (3%)
    unnamed x1, blocking collectives  69 us
    unnamed x3, waiting for transfers between devices  66.4 us
    all_to_all x1, waiting for transfers between devices, body(): lax.all_to_all(queries, 'ctx', split_axis=1, concat_axis=0, tiled=True)  45.5 us
    all_to_all x1, blocking collectives, sum_at_owner(): lax.all_to_all(pieces, axis, split_axis=0, concat_axis=0, tiled=True)  37.3 us
    all_to_all x1, waiting for transfers between devices, prepare_cards_here(): e_now = all_to_all(v_next, 'ctx', 0, 0)  25.2 us
    unnamed x34, local copies, waits for them, and re-layouts  17.8 us
    all_to_all x1, starting transfers between devices, prepare_cards_here(): e_now = all_to_all(v_next, 'ctx', 0, 0)  11.7 us
    dot_general x4, matrix products, query_block(): jnp.einsum('hqk,qhd->khd', rounded, grad_part, preferred_element_type=jnp...  10.5 us
  transfers between devices with their start and end apart: 7, of which 3 were waited for; matrix products, arithmetic and copies ran while one was open for 7% of the time, Pallas kernels for 0%

profile of v1, /device:TPU:8, one launch (start us, length us, event | category | flops | bytes accessed | tf_op | source)
XLA Modules:
  0.0 404.3 jit_solution(16161976742626323768)
XLA Ops:
  7.2 2.0 stack.2
  9.2 11.7 %all-to-all-start.2 = ((bf16[32,12,1024]{2,1,0:T(8,128)(2,1)}), bf16[32,12,1024]{2,1,0:T(8,128)(2,1)S(1)}, u32[]{:S(2)}, u32[]{:S(2)}) async-start(bf16[32,12,1024]{2,1,0:T(8,128)(2,1)} %stack.2), calls=%async_computation.2 | async-start | bytes 2097152 | tf_op jit(solution)/shard_map/all_to_all | solution.py:132
  20.9 2.4 copy.68
  23.4 25.2 %all-to-all-done.2 = bf16[32,12,1024]{2,1,0:T(8,128)(2,1)S(1)} async-done(((bf16[32,12,1024]{2,1,0:T(8,128)(2,1)}), bf16[32,12,1024]{2,1,0:T(8,128)(2,1)S(1)}, u32[]{:S(2)}, u32[]{:S(2)}) %all-to-all-start.2) | async-done | bytes 786464 | tf_op jit(solution)/shard_map/all_to_all | solution.py:132
  48.6 6.6 %all-to-all-start = ((bf16[128,32,256]{0,2,1:T(8,128)(2,1)}), bf16[128,32,256]{0,2,1:T(8,128)(2,1)S(1)}, u32[]{:S(2)}, u32[]{:S(2)}) async-start(bf16[128,32,256]{0,2,1:T(8,128)(2,1)} %bitcast.98), calls=%async_computation | async-start | bytes 4194304 | tf_op jit(solution)/shard_map/all_to_all | solution.py:146
  55.2 4.1 %copy.70 = bf16[128,8192]{0,1:T(8,128)(2,1)} copy(bf16[128,8192]{1,0:T(8,128)(2,1)} %param.10) | data formatting | bytes 4194304 | tf_op args[1]
  59.3 45.5 %all-to-all-done = bf16[128,32,256]{0,2,1:T(8,128)(2,1)S(1)} async-done(((bf16[128,32,256]{0,2,1:T(8,128)(2,1)}), bf16[128,32,256]{0,2,1:T(8,128)(2,1)S(1)}, u32[]{:S(2)}, u32[]{:S(2)}) %all-to-all-start) | async-done | bytes 2097184 | tf_op jit(solution)/shard_map/all_to_all | solution.py:146
  104.9 1.3 copy-done.4
  106.2 7.5 %all-to-all-start.3 = ((bf16[128,32,256]{0,2,1:T(8,128)(2,1)}), bf16[128,32,256]{0,2,1:T(8,128)(2,1)}, u32[]{:S(2)}, u32[]{:S(2)}) async-start(bf16[128,32,256]{0,2,1:T(8,128)(2,1)} %bitcast.96), calls=%async_computation.3 | async-start | bytes 4194304 | tf_op jit(solution)/shard_map/all_to_all | solution.py:147
  116.0 69.0 %all-reduce = s32[384]{0:T(512)S(1)} all-reduce(s32[384]{0:T(512)S(1)} %dynamic-update-slice), channel_id=1, replica_groups=mesh['dp'=8,'ctx'=32] {'ctx'}, use_global_device_ids=true, to_apply=%add | all-reduce | flops 384 | bytes 3072
  185.2 1.8 convolution_convert_fusion.3
  187.6 8.2 %all-to-all-start.1 = ((s32[32,1,128]{2,1,0:T(1,128)}), s32[32,1,128]{2,1,0:T(1,128)}, u32[]{:S(2)}, u32[]{:S(2)}) async-start(s32[32,1,128]{2,1,0:T(1,128)} %broadcast_in_dim.41), calls=%async_computation.1 | async-start | bytes 32768 | tf_op jit(solution)/shard_map/all_to_all | solution.py:22
  195.8 2.2 convolution_convert_fusion.4
  198.8 3.3 copy.69
  202.1 4.1 %copy.71 = bf16[128,32,256]{2,0,1:T(8,128)(2,1)} copy(bf16[128,32,256]{0,2,1:T(8,128)(2,1)} %all-to-all-done.3) | data formatting | bytes 4194304 | tf_op jit(solution)/shard_map/all_to_all | solution.py:147
  206.2 62.5 %while.27 = (s32[]{:T(128)}, f32[384,2,128]{0,2,1:T(8,128)S(1)}, f32[384,2,128]{0,2,1:T(8,128)}, bf16[4,1024,256]{2,1,0:T(8,128)(2,1)}, s32[4]{0:T(128)S(1)}, /*...) while((s32[]{:T(128)}, f32[384,2,128]{0,2,1:T(8,128)S(1)}, ...), condition=%wide.region_4.5_spmd.clone, body=%wide.region_0.4_spmd.clone.sunk | while | flops 1017117056 | bytes 58062732 | solution.py:110
  209.3 1.1 constant_dynamic-slice_fusion.3
  212.5 2.5 fusion.69
  215.0 2.5 fusion.71
  228.0 2.5 fusion.69
  230.6 2.7 fusion.71
  243.6 2.5 fusion.69
  246.2 2.7 fusion.71
  259.3 2.5 fusion.69
  261.9 2.7 fusion.71
  269.8 1.5 fusion.22
  271.9 37.3 %all_to_all.73 = bf16[32,12,1024]{2,1,0:T(8,128)(2,1)} all-to-all(bf16[32,12,1024]{2,1,0:T(8,128)(2,1)S(1)} %reshape.106), channel_id=1, replica_groups=mesh['dp'=8,'ctx'=32] {'ctx'}, dimensions={0} | all-to-all | bytes 1572864 | tf_op jit(solution)/shard_map/all_to_all | solution.py:46
  309.1 7.1 %all-to-all-start.4 = ((bf16[32,128,256]{2,1,0:T(8,128)(2,1)}), bf16[32,128,256]{2,1,0:T(8,128)(2,1)S(1)}, u32[]{:S(2)}, u32[]{:S(2)}) async-start(bf16[32,128,256]{2,1,0:T(8,128)(2,1)} %bitcast.101), calls=%async_computation.4 | async-start | bytes 4194304 | tf_op jit(solution)/shard_map/all_to_all | solution.py:153
  318.2 2.4 copy.86
  321.5 66.4 %reduce-scatter.4.cloned.1.call-done = bf16[128,512]{1,0:T(8,128)(2,1)} async-done(((bf16[1024,512]{1,0:T(8,128)(2,1)}), bf16[128,512]{1,0:T(8,128)(2,1)}) %reduce-scatter.4.cloned.1.call-update) | async-done | bytes 131088
  390.5 2.9 copy.76
  393.4 4.1 %copy.77 = bf16[128,8192]{1,0:T(8,128)(2,1)} copy(bf16[128,8192]{0,1:T(8,128)(2,1)} %bitcast.99) | data formatting | bytes 4194304
  (148 shorter events, 48.0 us)
Async XLA Ops:
  7.2 13.7 %copy-start.9 = (bf16[128,8192]{1,0:T(8,128)(2,1)S(1)}, bf16[128,8192]{1,0:T(8,128)(2,1)}, u32[]{:S(2)}) copy-start(bf16[128,8192]{1,0:T(8,128)(2,1)} %param.9) | copy-start | bytes 6291460
  9.2 39.4 %all-to-all-start.2 = ((bf16[32,12,1024]{2,1,0:T(8,128)(2,1)}), bf16[32,12,1024]{2,1,0:T(8,128)(2,1)S(1)}, u32[]{:S(2)}, u32[]{:S(2)}) async-start(bf16[32,12,1024]{2,1,0:T(8,128)(2,1)} %stack.2), calls=%async_computation.2 | async-start | bytes 2097152 | tf_op jit(solution)/shard_map/all_to_all | solution.py:132
  48.6 56.2 %all-to-all-start = ((bf16[128,32,256]{0,2,1:T(8,128)(2,1)}), bf16[128,32,256]{0,2,1:T(8,128)(2,1)S(1)}, u32[]{:S(2)}, u32[]{:S(2)}) async-start(bf16[128,32,256]{0,2,1:T(8,128)(2,1)} %bitcast.98), calls=%async_computation | async-start | bytes 4194304 | tf_op jit(solution)/shard_map/all_to_all | solution.py:146
  104.8 8.9 %copy-start.12 = (bf16[128,256]{1,0:T(8,128)(2,1)S(1)}, bf16[128,256]{1,0:T(8,128)(2,1)}, u32[]{:S(2)}) copy-start(bf16[128,256]{1,0:T(8,128)(2,1)} %param.13) | copy-start | bytes 196612
  104.8 8.9 %copy-start.13 = (bf16[128,256]{1,0:T(8,128)(2,1)S(1)}, bf16[128,256]{1,0:T(8,128)(2,1)}, u32[]{:S(2)}) copy-start(bf16[128,256]{1,0:T(8,128)(2,1)} %param.12) | copy-start | bytes 196612
  104.8 9.6 %copy-start.16 = (u32[256]{0:T(256)S(1)}, u32[256]{0:T(256)}, u32[]{:S(2)}) copy-start(u32[256]{0:T(256)} %constant.64) | copy-start | bytes 3076
  104.8 10.9 %copy-start.15 = (s32[12]{0:T(128)S(1)}, s32[12]{0:T(128)}, u32[]{:S(2)}) copy-start(s32[12]{0:T(128)} %param.15) | copy-start | bytes 148
  106.2 80.8 %all-to-all-start.3 = ((bf16[128,32,256]{0,2,1:T(8,128)(2,1)}), bf16[128,32,256]{0,2,1:T(8,128)(2,1)}, u32[]{:S(2)}, u32[]{:S(2)}) async-start(bf16[128,32,256]{0,2,1:T(8,128)(2,1)} %bitcast.96), calls=%async_computation.3 | async-start | bytes 4194304 | tf_op jit(solution)/shard_map/all_to_all | solution.py:147
  113.6 73.4 %copy-start.14 = (s32[128]{0:T(128)S(1)}, s32[128]{0:T(128)}, u32[]{:S(2)}) copy-start(s32[128]{0:T(128)} %param.14) | copy-start | bytes 1540
  113.6 71.5 %all-gather.2.cloned.1.call-start = ((), (), s32[]{:S(2)}) async-start(), calls=%async_computation.7 | async-start | bytes 1179648 | tf_op jit(solution)/shard_map/all_gather | solution.py:17
  185.2 12.9 %copy-start.5 = (bf16[384,1024]{1,0:T(8,128)(2,1)}, bf16[384,1024]{1,0:T(8,128)(2,1)S(1)}, u32[]{:S(2)}) copy-start(bf16[384,1024]{1,0:T(8,128)(2,1)S(1)} %reshape.103) | copy-start | bytes 2359300
  187.6 18.6 %all-to-all-start.1 = ((s32[32,1,128]{2,1,0:T(1,128)}), s32[32,1,128]{2,1,0:T(1,128)}, u32[]{:S(2)}, u32[]{:S(2)}) async-start(s32[32,1,128]{2,1,0:T(1,128)} %broadcast_in_dim.41), calls=%async_computation.1 | async-start | bytes 32768 | tf_op jit(solution)/shard_map/all_to_all | solution.py:22
  206.2 6.3 %copy-start.2 = (bf16[4096,256]{1,0:T(8,128)(2,1)}, bf16[4096,256]{1,0:T(8,128)(2,1)S(1)}, u32[]{:S(2)}) copy-start(bf16[4096,256]{1,0:T(8,128)(2,1)S(1)} %get-tuple-element.377) | copy-start | bytes 6291460 | tf_op jit(solution)/shard_map/while/body/eval_jaxpr/while
  215.0 2.6 copy-start.1
  215.0 2.6 copy-start.11
  220.1 1.6 copy-start.3
  221.7 6.3 %copy-start.2 = (bf16[4096,256]{1,0:T(8,128)(2,1)}, bf16[4096,256]{1,0:T(8,128)(2,1)S(1)}, u32[]{:S(2)}) copy-start(bf16[4096,256]{1,0:T(8,128)(2,1)S(1)} %get-tuple-element.377) | copy-start | bytes 6291460 | tf_op jit(solution)/shard_map/while/body/eval_jaxpr/while
  230.5 2.7 copy-start.1
  230.6 2.7 copy-start.11
  235.8 1.6 copy-start.3
  237.4 6.3 %copy-start.2 = (bf16[4096,256]{1,0:T(8,128)(2,1)}, bf16[4096,256]{1,0:T(8,128)(2,1)S(1)}, u32[]{:S(2)}) copy-start(bf16[4096,256]{1,0:T(8,128)(2,1)S(1)} %get-tuple-element.377) | copy-start | bytes 6291460 | tf_op jit(solution)/shard_map/while/body/eval_jaxpr/while
  246.2 2.7 copy-start.1
  246.2 2.7 copy-start.11
  253.0 6.3 %copy-start.2 = (bf16[4096,256]{1,0:T(8,128)(2,1)}, bf16[4096,256]{1,0:T(8,128)(2,1)S(1)}, u32[]{:S(2)}) copy-start(bf16[4096,256]{1,0:T(8,128)(2,1)S(1)} %get-tuple-element.377) | copy-start | bytes 6291460 | tf_op jit(solution)/shard_map/while/body/eval_jaxpr/while
  261.8 2.7 copy-start.1
  261.9 2.7 copy-start.11
  267.1 1.6 copy-start.3
  268.7 2.6 copy-start.10
  309.1 7.1 %copy-start.6 = (bf16[384,1024]{1,0:T(8,128)(2,1)S(1)}, bf16[384,1024]{1,0:T(8,128)(2,1)}, u32[]{:S(2)}) copy-start(bf16[384,1024]{1,0:T(8,128)(2,1)} %copy-done.5) | copy-start | bytes 2359300
  309.1 81.4 %all-to-all-start.4 = ((bf16[32,128,256]{2,1,0:T(8,128)(2,1)}), bf16[32,128,256]{2,1,0:T(8,128)(2,1)S(1)}, u32[]{:S(2)}, u32[]{:S(2)}) async-start(bf16[32,128,256]{2,1,0:T(8,128)(2,1)} %bitcast.101), calls=%async_computation.4 | async-start | bytes 4194304 | tf_op jit(solution)/shard_map/all_to_all | solution.py:153
  316.2 71.6 %reduce-scatter.4.cloned.1.call-start = ((), (), s32[]{:S(2)}) async-start(), calls=%async_computation.8 | async-start | bytes 1179648
  318.2 2.4 copy-start.8
  (10 other events, 10.8 us)
Sparse Core Ops, SparseCore 0:
  116.8 68.1 all-gather.1
  320.7 67.0 reduce-scatter.3
